TPU v7x, 32 devices: a whole 2x2x4 slice. The times are simulated.
32 devices in a mesh: region: 4 (over z), dev: 8 (over y, x, core).
Axes of the slice: x: 2, y: 2, z: 4, core: 2. Of those that a mesh axis runs over, the one named last changes fastest.
Arguments:
- loads: float32 [256, 32, 1024], P(('region', 'dev')), may hold values from -50 to 50
- factor: bfloat16 [256, 1024, 1024], P(('region', 'dev')), may hold values from -1 to 1, as said below
- pivots: float32 [256, 1024], P(('region', 'dev')), may hold values from 0.04 to 0.14, as said below
- lower: float32 [256, 1024], P(('region', 'dev')), may hold values from -1 to -0.2
- upper: float32 [256, 1024], P(('region', 'dev')), may hold values from 0.2 to 1
- incidence: int32 [256, 16], P(('region', 'dev')), may hold values from 0 to 511, as said below
- counts: int32 [256], P(('region', 'dev')), may hold values from 8 to 16, as said below
Outputs:
- dispatch: float32 [256, 32, 1024], P(('region', 'dev'))
- duals: float32 [256, 16, 128], P(('region', 'dev'))
- residuals: float32 [14, 2], replicated
Inputs may be any that keep to these rules, and one draw needn't show every extreme that they name: `incidence`: slot j of area a is live when j < counts[a]. Bus b is owned by device b // 16, devices numbered region-major. The live slots of one device name at most 16 buses owned by any one device of its own region and at most 8 buses owned in any one other region; in every draw every device reaches both bounds. A bus owned in another region is owned by the device with the same dev index there. `counts`: among the 8 areas of each device one has 16 live slots and the others at least 8. `factor`: unit lower triangular: ones on the diagonal, zeros above it. Rows below 64 of every area have inverse pivots of 0.10 or more; the other rows have them up to 0.14 as well.
All inputs are finite; a program needn't handle non-finite values.
Results may differ from a plain program's by a relative error of at most 0.005.
Values sent between devices are 32-bit elements; how exact they have to be, the bound alone decides.
A program may use at most 64 MiB of HBM per device.

v0:
```python
import jax
import jax.numpy as jnp
from jax import lax
from jax.sharding import PartitionSpec as P

ROWS_SLOT = 4
BLK = 128
BUS_DEV = 16
CAP_X = 8
ITERS = 14


RHO = 4.0
SIGMA = 1.0
HIGH = lax.Precision.HIGHEST


def to_blocks(state_field, slot_count, row_group):
    area_count, scenarios, system_order = state_field.shape
    leading = state_field[:, :, : slot_count * row_group].reshape(
        area_count, scenarios, slot_count, row_group
    )
    return jnp.transpose(leading, (0, 2, 1, 3)).reshape(
        area_count, slot_count, scenarios * row_group
    )


def from_blocks(blocks, scenarios, row_group, system_order):
    area_count, slot_count, block_values = blocks.shape
    leading = jnp.transpose(
        blocks.reshape(area_count, slot_count, scenarios, row_group), (0, 2, 1, 3)
    )
    leading = leading.reshape(area_count, scenarios, slot_count * row_group)
    return jnp.pad(leading, ((0, 0), (0, 0), (0, system_order - slot_count * row_group)))


def apply_inverse(right_side, factor, pivots, block_width):
    rounded = right_side.astype(jnp.bfloat16)
    system_order = factor.shape[1]
    block_count = system_order // block_width
    pieces = []
    for index_row in range(block_count):
        finish = (index_row + 1) * block_width
        pieces.append(
            jnp.einsum(
                "ask,aik->asi",
                rounded[:, :, :finish],
                factor[:, index_row * block_width : finish, :finish],
                preferred_element_type=jnp.float32,
            )
        )
    forward = jnp.concatenate(pieces, axis=2)
    scaled = (forward * pivots[:, None, :]).astype(jnp.bfloat16)
    results = []
    for index_col in range(block_count):
        begin = index_col * block_width
        results.append(
            jnp.einsum(
                "asi,aik->ask",
                scaled[:, :, begin:],
                factor[:, begin:, begin : begin + block_width],
                preferred_element_type=jnp.float32,
            )
        )
    return jnp.concatenate(results, axis=2)


def select(selector, values):
    return jnp.dot(selector, values, precision=HIGH, preferred_element_type=jnp.float32)


def on_device(loads, factor, pivots, lower, upper, incidence, counts):
    area_count, scenarios, system_order = loads.shape
    slot_count = incidence.shape[1]
    item_count = area_count * slot_count
    block_values = scenarios * ROWS_SLOT
    n_dev = lax.axis_size("dev")
    n_region = lax.axis_size("region")
    cap_near = max(item_count // n_dev, 2)
    my_region = lax.axis_index("region")
    live_slot = (jnp.arange(slot_count)[None, :] < counts[:, None]).reshape(item_count)
    bus_ids = incidence.reshape(item_count)
    owner_dev = bus_ids // BUS_DEV
    owner_region = owner_dev // n_dev
    owner_peer = owner_dev % n_dev
    near_live = live_slot & (owner_region == my_region)
    far_live = live_slot & (owner_region != my_region)
    earlier = jnp.arange(item_count)[None, :] < jnp.arange(item_count)[:, None]
    rank_near = jnp.sum(
        near_live[None, :] & (owner_peer[None, :] == owner_peer[:, None]) & earlier, axis=1
    )
    rank_far = jnp.sum(
        far_live[None, :] & (owner_region[None, :] == owner_region[:, None]) & earlier, axis=1
    )
    slot_near = jnp.where(near_live, owner_peer * cap_near + rank_near, -1)
    slot_far = jnp.where(far_live, owner_region * CAP_X + rank_far, -1)
    near_hits = jnp.arange(n_dev * cap_near)[:, None] == slot_near[None, :]
    far_hits = jnp.arange(n_region * CAP_X)[:, None] == slot_far[None, :]
    pick_near = near_hits.astype(jnp.float32)
    pick_far = far_hits.astype(jnp.float32)
    far_tags = jnp.sum(jnp.where(far_hits, bus_ids[None, :] + 1, 0), axis=1) - 1
    got_far_tags = lax.all_to_all(far_tags, "region", split_axis=0, concat_axis=0, tiled=True)
    near_tags = jnp.sum(jnp.where(near_hits, bus_ids[None, :] + 1, 0), axis=1) - 1
    got_near_tags = lax.all_to_all(near_tags, "dev", split_axis=0, concat_axis=0, tiled=True)
    listed_tags = jnp.concatenate([got_near_tags, got_far_tags])
    same_bus = (
        (listed_tags[:, None] == listed_tags[None, :]) & (listed_tags[:, None] >= 0)
    ).astype(jnp.float32)
    far_start = n_dev * cap_near
    members = jnp.maximum(jnp.sum(same_bus, axis=1), 1.0)
    live_col = live_slot.astype(jnp.float32)[:, None]
    floor_box = lower[:, None, :]
    ceil_box = upper[:, None, :]
    total_cells = float(area_count * n_dev * n_region * block_values)

    def iterate(step_num, state_now):
        dispatch, clipped, offset, duals, z_slot, z_prev, record = state_now
        pushed = from_blocks(
            ((z_slot - duals) * live_col).reshape(area_count, slot_count, block_values),
            scenarios,
            ROWS_SLOT,
            system_order,
        )
        right_side = loads + RHO * pushed + SIGMA * (clipped - offset)
        dispatch = apply_inverse(right_side, factor, pivots, BLK)
        clipped_new = jnp.clip(dispatch + offset, floor_box, ceil_box)
        offset = offset + dispatch - clipped_new
        blocks = to_blocks(dispatch, slot_count, ROWS_SLOT).reshape(item_count, block_values)
        values = (blocks + duals) * live_col
        got_far = lax.all_to_all(
            select(pick_far, values), "region", split_axis=0, concat_axis=0, tiled=True
        )
        got_near = lax.all_to_all(
            select(pick_near, values), "dev", split_axis=0, concat_axis=0, tiled=True
        )
        z_list = select(same_bus, jnp.concatenate([got_near, got_far])) / members[:, None]
        back_near = lax.all_to_all(
            z_list[:far_start], "dev", split_axis=0, concat_axis=0, tiled=True
        )
        near_part = select(pick_near.T, back_near)
        back_far = lax.all_to_all(
            z_list[far_start:], "region", split_axis=0, concat_axis=0, tiled=True
        )
        z_slot = near_part + select(pick_far.T, back_far)
        misfit = (blocks - z_slot) * live_col
        duals = duals + misfit
        change = z_list - z_prev
        partial_value = (
            jnp.stack(
                [jnp.sum(misfit * misfit), RHO * RHO * jnp.sum(change * change / members[:, None])]
            )
            / total_cells
        )
        partial_value = lax.psum(partial_value, ("region", "dev"))
        record = record.at[step_num].set(partial_value)
        return (dispatch, clipped_new, offset, duals, z_slot, z_list, record)

    start_state = (
        jnp.zeros_like(loads),
        jnp.zeros_like(loads),
        jnp.zeros_like(loads),
        jnp.zeros((item_count, block_values), jnp.float32),
        jnp.zeros((item_count, block_values), jnp.float32),
        jnp.zeros((same_bus.shape[0], block_values), jnp.float32),
        jnp.zeros((ITERS, 2), jnp.float32),
    )
    final_state = lax.fori_loop(0, ITERS, iterate, start_state)
    dispatch = final_state[0]
    duals = final_state[3].reshape(area_count, slot_count, block_values)
    record = final_state[6]
    return (dispatch, duals, record)


def solution(mesh):
    placed = (
        P(("region", "dev"), None, None),
        P(("region", "dev"), None, None),
        P(("region", "dev"), None),
        P(("region", "dev"), None),
        P(("region", "dev"), None),
        P(("region", "dev"), None),
        P(("region", "dev")),
    )
    return jax.shard_map(
        on_device,
        mesh=mesh,
        in_specs=placed,
        out_specs=(P(("region", "dev"), None, None), P(("region", "dev"), None, None), P()),
        check_vma=False,
    )
```

profile of v0, /device:TPU:0, one launch (start us, length us, event | category | flops | bytes accessed | tf_op | source)
XLA Modules:
  0.0 1641.5 jit_solution(15313807213250353400)
XLA Ops:
  3.6 6.3 all-to-all-start.5
  31.6 1607.8 %while.29 = (s32[]{:T(128)}, f32[8,32,1024]{2,1,0:T(8,128)}, f32[8,32,1024]{2,1,0:T(8,128)}, f32[8,32,1024]{2,1,0:T(8,128)S(1)}, f32[128,128]{0,1:T(8,128)S(1)},...) while((s32[]{:T(128)}, f32[8,32,1024]{2,1,0:T(8,128)}, ...), condition=%wide.region_10.11_spmd.clone, body=%wide.region_5.10_spmd.clone.sunk | while | flops 710429952 | bytes 42458640 | solution.py:167
  97.4 5.3 all-to-all-done.3
  105.0 38.3 %psum.16 = f32[1,2]{1,0:T(1,128)S(1)} all-reduce(f32[1,2]{1,0:T(1,128)S(1)} %fusion.200), channel_id=1, replica_groups=mesh['region'=4,'dev'=8] {'region','dev'}, use_global_device_ids=true, to_apply=%region_9.9 | all-reduce | flops 2 | bytes 16 | tf_op jit(solution)/shard_map/while/body/eval_jaxpr/psum | solution.py:154
  212.3 5.3 all-to-all-done.3
  219.9 38.3 %psum.16 = f32[1,2]{1,0:T(1,128)S(1)} all-reduce(f32[1,2]{1,0:T(1,128)S(1)} %fusion.200), channel_id=1, replica_groups=mesh['region'=4,'dev'=8] {'region','dev'}, use_global_device_ids=true, to_apply=%region_9.9 | all-reduce | flops 2 | bytes 16 | tf_op jit(solution)/shard_map/while/body/eval_jaxpr/psum | solution.py:154
  327.1 5.3 all-to-all-done.3
  334.8 38.3 %psum.16 = f32[1,2]{1,0:T(1,128)S(1)} all-reduce(f32[1,2]{1,0:T(1,128)S(1)} %fusion.200), channel_id=1, replica_groups=mesh['region'=4,'dev'=8] {'region','dev'}, use_global_device_ids=true, to_apply=%region_9.9 | all-reduce | flops 2 | bytes 16 | tf_op jit(solution)/shard_map/while/body/eval_jaxpr/psum | solution.py:154
  442.0 5.3 all-to-all-done.3
  449.7 38.3 %psum.16 = f32[1,2]{1,0:T(1,128)S(1)} all-reduce(f32[1,2]{1,0:T(1,128)S(1)} %fusion.200), channel_id=1, replica_groups=mesh['region'=4,'dev'=8] {'region','dev'}, use_global_device_ids=true, to_apply=%region_9.9 | all-reduce | flops 2 | bytes 16 | tf_op jit(solution)/shard_map/while/body/eval_jaxpr/psum | solution.py:154
  556.9 5.3 all-to-all-done.3
  564.6 38.3 %psum.16 = f32[1,2]{1,0:T(1,128)S(1)} all-reduce(f32[1,2]{1,0:T(1,128)S(1)} %fusion.200), channel_id=1, replica_groups=mesh['region'=4,'dev'=8] {'region','dev'}, use_global_device_ids=true, to_apply=%region_9.9 | all-reduce | flops 2 | bytes 16 | tf_op jit(solution)/shard_map/while/body/eval_jaxpr/psum | solution.py:154
  671.8 5.3 all-to-all-done.3
  679.5 38.3 %psum.16 = f32[1,2]{1,0:T(1,128)S(1)} all-reduce(f32[1,2]{1,0:T(1,128)S(1)} %fusion.200), channel_id=1, replica_groups=mesh['region'=4,'dev'=8] {'region','dev'}, use_global_device_ids=true, to_apply=%region_9.9 | all-reduce | flops 2 | bytes 16 | tf_op jit(solution)/shard_map/while/body/eval_jaxpr/psum | solution.py:154
  786.7 5.3 all-to-all-done.3
  794.4 38.3 %psum.16 = f32[1,2]{1,0:T(1,128)S(1)} all-reduce(f32[1,2]{1,0:T(1,128)S(1)} %fusion.200), channel_id=1, replica_groups=mesh['region'=4,'dev'=8] {'region','dev'}, use_global_device_ids=true, to_apply=%region_9.9 | all-reduce | flops 2 | bytes 16 | tf_op jit(solution)/shard_map/while/body/eval_jaxpr/psum | solution.py:154
  901.6 5.3 all-to-all-done.3
  909.3 38.3 %psum.16 = f32[1,2]{1,0:T(1,128)S(1)} all-reduce(f32[1,2]{1,0:T(1,128)S(1)} %fusion.200), channel_id=1, replica_groups=mesh['region'=4,'dev'=8] {'region','dev'}, use_global_device_ids=true, to_apply=%region_9.9 | all-reduce | flops 2 | bytes 16 | tf_op jit(solution)/shard_map/while/body/eval_jaxpr/psum | solution.py:154
  1024.2 38.3 %psum.16 = f32[1,2]{1,0:T(1,128)S(1)} all-reduce(f32[1,2]{1,0:T(1,128)S(1)} %fusion.200), channel_id=1, replica_groups=mesh['region'=4,'dev'=8] {'region','dev'}, use_global_device_ids=true, to_apply=%region_9.9 | all-reduce | flops 2 | bytes 16 | tf_op jit(solution)/shard_map/while/body/eval_jaxpr/psum | solution.py:154
  1139.0 38.3 %psum.16 = f32[1,2]{1,0:T(1,128)S(1)} all-reduce(f32[1,2]{1,0:T(1,128)S(1)} %fusion.200), channel_id=1, replica_groups=mesh['region'=4,'dev'=8] {'region','dev'}, use_global_device_ids=true, to_apply=%region_9.9 | all-reduce | flops 2 | bytes 16 | tf_op jit(solution)/shard_map/while/body/eval_jaxpr/psum | solution.py:154
  1253.9 38.3 %psum.16 = f32[1,2]{1,0:T(1,128)S(1)} all-reduce(f32[1,2]{1,0:T(1,128)S(1)} %fusion.200), channel_id=1, replica_groups=mesh['region'=4,'dev'=8] {'region','dev'}, use_global_device_ids=true, to_apply=%region_9.9 | all-reduce | flops 2 | bytes 16 | tf_op jit(solution)/shard_map/while/body/eval_jaxpr/psum | solution.py:154
  1368.8 38.3 %psum.16 = f32[1,2]{1,0:T(1,128)S(1)} all-reduce(f32[1,2]{1,0:T(1,128)S(1)} %fusion.200), channel_id=1, replica_groups=mesh['region'=4,'dev'=8] {'region','dev'}, use_global_device_ids=true, to_apply=%region_9.9 | all-reduce | flops 2 | bytes 16 | tf_op jit(solution)/shard_map/while/body/eval_jaxpr/psum | solution.py:154
  1483.7 38.3 %psum.16 = f32[1,2]{1,0:T(1,128)S(1)} all-reduce(f32[1,2]{1,0:T(1,128)S(1)} %fusion.200), channel_id=1, replica_groups=mesh['region'=4,'dev'=8] {'region','dev'}, use_global_device_ids=true, to_apply=%region_9.9 | all-reduce | flops 2 | bytes 16 | tf_op jit(solution)/shard_map/while/body/eval_jaxpr/psum | solution.py:154
  1598.5 38.3 %psum.16 = f32[1,2]{1,0:T(1,128)S(1)} all-reduce(f32[1,2]{1,0:T(1,128)S(1)} %fusion.200), channel_id=1, replica_groups=mesh['region'=4,'dev'=8] {'region','dev'}, use_global_device_ids=true, to_apply=%region_9.9 | all-reduce | flops 2 | bytes 16 | tf_op jit(solution)/shard_map/while/body/eval_jaxpr/psum | solution.py:154
  (773 shorter events, 1045.1 us)
Async XLA Ops:
  3.6 11.8 all-to-all-start.5
  53.9 17.5 %all-to-all-start = ((f32[4,8,128]{2,1,0:T(8,128)}), f32[4,8,128]{2,1,0:T(8,128)S(1)}, u32[]{:S(2)}, u32[]{:S(2)}) async-start(f32[4,8,128]{2,1,0:T(8,128)} %convolution_bitcast_fusion.2), calls=%async_computation | async-start | bytes 32768 | tf_op jit(solution)/shard_map/while/body/eval_jaxpr/all_to_all | solution.py:130
  92.0 10.7 all-to-all-start.3
  168.5 17.5 %all-to-all-start = ((f32[4,8,128]{2,1,0:T(8,128)}), f32[4,8,128]{2,1,0:T(8,128)S(1)}, u32[]{:S(2)}, u32[]{:S(2)}) async-start(f32[4,8,128]{2,1,0:T(8,128)} %convolution_bitcast_fusion.2), calls=%async_computation | async-start | bytes 32768 | tf_op jit(solution)/shard_map/while/body/eval_jaxpr/all_to_all | solution.py:130
  206.9 10.7 all-to-all-start.3
  283.4 17.5 %all-to-all-start = ((f32[4,8,128]{2,1,0:T(8,128)}), f32[4,8,128]{2,1,0:T(8,128)S(1)}, u32[]{:S(2)}, u32[]{:S(2)}) async-start(f32[4,8,128]{2,1,0:T(8,128)} %convolution_bitcast_fusion.2), calls=%async_computation | async-start | bytes 32768 | tf_op jit(solution)/shard_map/while/body/eval_jaxpr/all_to_all | solution.py:130
  321.8 10.7 all-to-all-start.3
  398.3 17.5 %all-to-all-start = ((f32[4,8,128]{2,1,0:T(8,128)}), f32[4,8,128]{2,1,0:T(8,128)S(1)}, u32[]{:S(2)}, u32[]{:S(2)}) async-start(f32[4,8,128]{2,1,0:T(8,128)} %convolution_bitcast_fusion.2), calls=%async_computation | async-start | bytes 32768 | tf_op jit(solution)/shard_map/while/body/eval_jaxpr/all_to_all | solution.py:130
  436.7 10.7 all-to-all-start.3
  513.2 17.5 %all-to-all-start = ((f32[4,8,128]{2,1,0:T(8,128)}), f32[4,8,128]{2,1,0:T(8,128)S(1)}, u32[]{:S(2)}, u32[]{:S(2)}) async-start(f32[4,8,128]{2,1,0:T(8,128)} %convolution_bitcast_fusion.2), calls=%async_computation | async-start | bytes 32768 | tf_op jit(solution)/shard_map/while/body/eval_jaxpr/all_to_all | solution.py:130
  628.1 17.5 %all-to-all-start = ((f32[4,8,128]{2,1,0:T(8,128)}), f32[4,8,128]{2,1,0:T(8,128)S(1)}, u32[]{:S(2)}, u32[]{:S(2)}) async-start(f32[4,8,128]{2,1,0:T(8,128)} %convolution_bitcast_fusion.2), calls=%async_computation | async-start | bytes 32768 | tf_op jit(solution)/shard_map/while/body/eval_jaxpr/all_to_all | solution.py:130
  743.0 17.5 %all-to-all-start = ((f32[4,8,128]{2,1,0:T(8,128)}), f32[4,8,128]{2,1,0:T(8,128)S(1)}, u32[]{:S(2)}, u32[]{:S(2)}) async-start(f32[4,8,128]{2,1,0:T(8,128)} %convolution_bitcast_fusion.2), calls=%async_computation | async-start | bytes 32768 | tf_op jit(solution)/shard_map/while/body/eval_jaxpr/all_to_all | solution.py:130
  857.9 17.5 %all-to-all-start = ((f32[4,8,128]{2,1,0:T(8,128)}), f32[4,8,128]{2,1,0:T(8,128)S(1)}, u32[]{:S(2)}, u32[]{:S(2)}) async-start(f32[4,8,128]{2,1,0:T(8,128)} %convolution_bitcast_fusion.2), calls=%async_computation | async-start | bytes 32768 | tf_op jit(solution)/shard_map/while/body/eval_jaxpr/all_to_all | solution.py:130
  972.8 17.5 %all-to-all-start = ((f32[4,8,128]{2,1,0:T(8,128)}), f32[4,8,128]{2,1,0:T(8,128)S(1)}, u32[]{:S(2)}, u32[]{:S(2)}) async-start(f32[4,8,128]{2,1,0:T(8,128)} %convolution_bitcast_fusion.2), calls=%async_computation | async-start | bytes 32768 | tf_op jit(solution)/shard_map/while/body/eval_jaxpr/all_to_all | solution.py:130
  1087.6 17.5 %all-to-all-start = ((f32[4,8,128]{2,1,0:T(8,128)}), f32[4,8,128]{2,1,0:T(8,128)S(1)}, u32[]{:S(2)}, u32[]{:S(2)}) async-start(f32[4,8,128]{2,1,0:T(8,128)} %convolution_bitcast_fusion.2), calls=%async_computation | async-start | bytes 32768 | tf_op jit(solution)/shard_map/while/body/eval_jaxpr/all_to_all | solution.py:130
  1126.0 10.7 all-to-all-start.3
  1202.5 17.5 %all-to-all-start = ((f32[4,8,128]{2,1,0:T(8,128)}), f32[4,8,128]{2,1,0:T(8,128)S(1)}, u32[]{:S(2)}, u32[]{:S(2)}) async-start(f32[4,8,128]{2,1,0:T(8,128)} %convolution_bitcast_fusion.2), calls=%async_computation | async-start | bytes 32768 | tf_op jit(solution)/shard_map/while/body/eval_jaxpr/all_to_all | solution.py:130
  1240.9 10.7 all-to-all-start.3
  1317.4 17.5 %all-to-all-start = ((f32[4,8,128]{2,1,0:T(8,128)}), f32[4,8,128]{2,1,0:T(8,128)S(1)}, u32[]{:S(2)}, u32[]{:S(2)}) async-start(f32[4,8,128]{2,1,0:T(8,128)} %convolution_bitcast_fusion.2), calls=%async_computation | async-start | bytes 32768 | tf_op jit(solution)/shard_map/while/body/eval_jaxpr/all_to_all | solution.py:130
  1355.8 10.7 all-to-all-start.3
  1432.3 17.5 %all-to-all-start = ((f32[4,8,128]{2,1,0:T(8,128)}), f32[4,8,128]{2,1,0:T(8,128)S(1)}, u32[]{:S(2)}, u32[]{:S(2)}) async-start(f32[4,8,128]{2,1,0:T(8,128)} %convolution_bitcast_fusion.2), calls=%async_computation | async-start | bytes 32768 | tf_op jit(solution)/shard_map/while/body/eval_jaxpr/all_to_all | solution.py:130
  1470.7 10.7 all-to-all-start.3
  1547.2 17.5 %all-to-all-start = ((f32[4,8,128]{2,1,0:T(8,128)}), f32[4,8,128]{2,1,0:T(8,128)S(1)}, u32[]{:S(2)}, u32[]{:S(2)}) async-start(f32[4,8,128]{2,1,0:T(8,128)} %convolution_bitcast_fusion.2), calls=%async_computation | async-start | bytes 32768 | tf_op jit(solution)/shard_map/while/body/eval_jaxpr/all_to_all | solution.py:130
  1585.5 10.7 all-to-all-start.3
  (76 other events, 2148.4 us)
where the time goes:
time: 1660 us; the launch traced here: 1640 us
  blocking collectives  536 us (32%)
  matrix products  467 us (28%)
  starting transfers between devices  223 us (13%)
  waiting for transfers between devices  185 us (11%)
  other arithmetic  130 us (8%)
  local copies, waits for them, and re-layouts  89.1 us (5%)
    psum x14, blocking collectives, iterate(): partial_value = lax.psum(partial_value, ('region', 'dev'))  536 us
    dot_general x112, matrix products, apply_inverse(): jnp.einsum('ask,aik->asi', rounded[:, :, :finish], factor[:, index_row *...  202 us
    dot_general x112, matrix products, apply_inverse(): jnp.einsum('asi,aik->ask', scaled[:, :, begin:], factor[:, begin:, begin:...  180 us
    dot_general x70, matrix products, select(): jnp.dot(selector, values, precision=HIGH, preferred_element_type=jnp.floa...  85.2 us
    all_to_all x14, waiting for transfers between devices, iterate(): lax.all_to_all(z_list[far_start:], 'region', split_axis=0, concat_axis=0,...  74.5 us
    all_to_all x14, starting transfers between devices, iterate(): lax.all_to_all(z_list[far_start:], 'region', split_axis=0, concat_axis=0,...  70.7 us
    all_to_all x14, waiting for transfers between devices, iterate(): lax.all_to_all(select(pick_near, values), 'dev', split_axis=0, concat_axi...  59.8 us
    all_to_all x14, starting transfers between devices, iterate(): lax.all_to_all(select(pick_near, values), 'dev', split_axis=0, concat_axi...  49.6 us
  transfers between devices with their start and end apart: 58, of which 44 were waited for; matrix products, arithmetic and copies ran while one was open for 14% of the time, Pallas kernels for 0%

commit v1 on v0

v1 whole, which is shorter than its diff:
```python
import functools

import jax
import jax.numpy as jnp
from jax import lax
from jax.experimental import pallas as pl
from jax.experimental.pallas import tpu as pltpu
from jax.sharding import PartitionSpec as P

ROWS_SLOT = 4
BLK = 128
BUS_DEV = 16
ITERS = 14
RHO = 4.0
SIGMA = 1.0
TILE = 256
F32 = jnp.float32
BF16 = jnp.bfloat16
MESH = pl.DeviceIdType.MESH
NT = (((1,), (1,)), ((), ()))
NN = (((1,), (0,)), ((), ()))


def mm(left, right, dims=NN):
    return lax.dot_general(left, right, dims, preferred_element_type=F32)


def split3(x):
    high = x.astype(BF16)
    rest = x - high.astype(F32)
    mid = rest.astype(BF16)
    low = (rest - mid.astype(F32)).astype(BF16)
    return high, mid, low


def kernel(
    n_region, n_dev, area_count, scenarios, order, slots,
    loads_ref, factor_ref, pivots_ref, lower_ref, upper_ref, row_ref, col_ref,
    dispatch_ref, duals_ref, res_ref,
    fac, wide, known, scaled, offset, pick, place, live, rhs_b, base_b, off_b, loads_b, low_b, up_b, blk, duals,
    part, got, table, mean, counts_got, members, res_sum, res_near, res_far,
    fac_sem, send_sem, back_send, got_sem, table_sem, counts_sem, near_sem, far_sem,
):
    me_r = lax.axis_index("region")
    me_d = lax.axis_index("dev")
    items = area_count * slots
    rows = area_count * scenarios
    places = ROWS_SLOT * items
    edge = slots * ROWS_SLOT
    groups = n_dev + n_region
    near = [lax.rem(me_d + step, n_dev) for step in range(1, n_dev)]
    far = [lax.rem(me_r + step, n_region) for step in range(1, n_region)]
    peers = [((me_r, d), d, me_d, d) for d in near]
    peers += [((r, me_d), n_dev + r, n_dev + me_r, n_dev + r) for r in far]

    def factor_copy(area):
        return pltpu.make_async_copy(factor_ref.at[area], fac.at[area], fac_sem.at[area])

    for area in range(area_count):
        factor_copy(area).start()

    got[...] = jnp.zeros_like(got)
    counts_got[...] = jnp.zeros_like(counts_got)
    table[...] = jnp.zeros_like(table)
    res_sum[...] = jnp.zeros_like(res_sum)

    barrier = pltpu.get_barrier_semaphore()
    for device, _, _, _ in peers:
        pl.semaphore_signal(barrier, inc=1, device_id=device, device_id_type=MESH)
    pl.semaphore_wait(barrier, len(peers))

    def group_rows(index):
        return pl.ds(pl.multiple_of(index * BUS_DEV, BUS_DEV), BUS_DEV)

    def outgoing(number, target, semaphores):
        device, theirs, mine, _ = peers[number]
        return pltpu.make_async_remote_copy(
            src_ref=part.at[group_rows(theirs)], dst_ref=target.at[group_rows(mine)],
            send_sem=send_sem.at[number], recv_sem=semaphores.at[mine],
            device_id=device, device_id_type=MESH,
        )

    def incoming(number, target, semaphores):
        device, theirs, _, here = peers[number]
        return pltpu.make_async_remote_copy(
            src_ref=part.at[group_rows(theirs)], dst_ref=target.at[group_rows(here)],
            send_sem=send_sem.at[number], recv_sem=semaphores.at[here],
            device_id=device, device_id_type=MESH,
        )

    def back(number, here=False):
        device, _, mine, theirs = peers[number]
        at = theirs if here else mine
        return pltpu.make_async_remote_copy(
            src_ref=mean, dst_ref=table.at[group_rows(at)],
            send_sem=back_send.at[number], recv_sem=table_sem.at[at],
            device_id=device, device_id_type=MESH,
        )

    def group_sum(ref):
        total = ref[0:BUS_DEV, :]
        for index in range(1, groups):
            total = total + ref[index * BUS_DEV : (index + 1) * BUS_DEV, :]
        return total

    picked = lax.broadcasted_iota(jnp.int32, (groups * BUS_DEV, items), 0) == row_ref[...]
    picked = jnp.where(picked, 1.0, 0.0)
    part[...] = jnp.broadcast_to(jnp.sum(picked, axis=1, keepdims=True), part.shape)
    for number in range(len(peers)):
        outgoing(number, counts_got, counts_sem).start()
    pick[...] = picked.astype(BF16)
    placed = lax.broadcasted_iota(jnp.int32, (items, groups * BUS_DEV), 1) == col_ref[...]
    place[...] = jnp.where(placed, 1.0, 0.0).astype(BF16)
    live[...] = jnp.broadcast_to(jnp.where(col_ref[...] >= 0, 1.0, 0.0), live.shape)
    counts_got[group_rows(me_d), :] = part[group_rows(me_d), :]

    source = lax.broadcasted_iota(jnp.int32, (area_count * BLK, places), 0)
    target = lax.broadcasted_iota(jnp.int32, (area_count * BLK, places), 1)
    slot_of = lax.rem(target, slots)
    area_of = lax.rem(target // slots, area_count)
    row_of = target // items
    order_hot = jnp.where(source == area_of * BLK + slot_of * ROWS_SLOT + row_of, 1.0, 0.0).astype(BF16)

    def stack_rows(x):
        return jnp.concatenate([x[:, r * items : (r + 1) * items] for r in range(ROWS_SLOT)], axis=0)

    def to_blocks(x):
        parts = [mm(piece, order_hot) for piece in split3(x)]
        return stack_rows(parts[0] + parts[1] + parts[2]).T

    loads_b[...] = to_blocks(jnp.concatenate([loads_ref[a, :, :BLK] for a in range(area_count)], axis=1))
    for bound, kept in ((lower_ref, low_b), (upper_ref, up_b)):
        line = jnp.concatenate([bound[a : a + 1, :BLK] for a in range(area_count)], axis=1)
        kept[...] = to_blocks(jnp.broadcast_to(line, (scenarios, area_count * BLK)))

    column = lax.broadcasted_iota(jnp.int32, (scenarios, TILE), 1)
    tiles = order // TILE

    def forward_known(area, pieces):
        for c in range(tiles):
            here = jnp.concatenate(pieces[: c + 1], axis=1) if c else pieces[0]
            known[pl.ds(area * scenarios, scenarios), c * TILE : (c + 1) * TILE] = mm(
                here, fac[area, c * TILE : (c + 1) * TILE, : (c + 1) * TILE], NT
            )

    def first(area, carry):
        factor_copy(area).wait()
        pieces = []
        for c in range(tiles):
            value = loads_ref[area, :, c * TILE : (c + 1) * TILE]
            if c == 0:
                value = jnp.where(column < edge, 0.0, value)
            pieces.append(value.astype(BF16))
        forward_known(area, pieces)
        return carry

    lax.fori_loop(0, area_count, first, 0)

    def gather_wide(chunk, carry):
        at = pl.ds(pl.multiple_of(chunk * TILE, TILE), TILE)
        joined = jnp.concatenate([fac[a, at, :BLK] for a in range(area_count)], axis=1)
        wide[at, :] = mm(joined, order_hot).astype(BF16)
        return carry

    lax.fori_loop(0, tiles, gather_wide, 0)

    offset[...] = jnp.zeros_like(offset)
    off_b[...] = jnp.zeros_like(off_b)
    duals[...] = jnp.zeros_like(duals)
    mean[...] = jnp.zeros_like(mean)
    rhs_b[...] = loads_b[...]

    for number in range(len(peers)):
        incoming(number, counts_got, counts_sem).wait_recv()
        outgoing(number, counts_got, counts_sem).wait_send()
    members[...] = jnp.maximum(group_sum(counts_got), 1.0)

    own_area = lax.broadcasted_iota(jnp.int32, (scenarios, places), 1)
    own_area = lax.rem(own_area // slots, area_count)

    def interior(area, carry):
        at = pl.ds(pl.multiple_of(area * scenarios, scenarios), scenarios)
        pieces = []
        for c in range(tiles):
            cols = slice(c * TILE, (c + 1) * TILE)
            found = mm(scaled[at, c * TILE :], fac[area, c * TILE :, cols])
            dispatch_ref[area, :, cols] = found
            moved = found + offset[at, cols]
            boxed = jnp.clip(moved, lower_ref[pl.ds(area, 1), cols], upper_ref[pl.ds(area, 1), cols])
            rest = moved - boxed
            offset[at, cols] = rest
            value = loads_ref[area, :, cols] + SIGMA * (boxed - rest)
            if c == 0:
                value = jnp.where(column < edge, 0.0, value)
            pieces.append(value.astype(BF16))
        forward_known(area, pieces)
        return carry

    def iterate(step, carry):
        turned = rhs_b[...].T
        flat = jnp.concatenate(
            [turned[r * scenarios : (r + 1) * scenarios, :] for r in range(ROWS_SLOT)], axis=1
        )
        left = jnp.concatenate(
            [jnp.where(own_area == a, flat, 0.0) for a in range(area_count)], axis=0
        ).astype(BF16)
        for c in range(tiles):
            cols = slice(c * TILE, (c + 1) * TILE)
            forward = known[:, cols] + mm(left, wide[cols, :], NT)
            forward = forward.reshape(area_count, scenarios, TILE) * pivots_ref[:, cols][:, None, :]
            scaled[:, cols] = forward.reshape(rows, TILE).astype(BF16)
        product = mm(scaled[...], wide[...])
        total = jnp.zeros((scenarios, places), F32)
        for a in range(area_count):
            total = total + jnp.where(own_area == a, product[a * scenarios : (a + 1) * scenarios, :], 0.0)
        block = stack_rows(total).T
        blk[...] = block
        values = (block + duals[...]) * live[...]
        pieces = split3(values)
        part[...] = mm(pick[...], pieces[0]) + mm(pick[...], pieces[1]) + mm(pick[...], pieces[2])
        for number in range(len(peers)):
            outgoing(number, got, got_sem).start()
        got[group_rows(me_d), :] = part[group_rows(me_d), :]
        moved = block + off_b[...]
        boxed = jnp.clip(moved, low_b[...], up_b[...])
        rest = moved - boxed
        off_b[...] = rest
        base_b[...] = loads_b[...] + SIGMA * (boxed - rest)

        lax.fori_loop(0, area_count // 2, interior, 0)

        for number in range(len(peers)):
            incoming(number, got, got_sem).wait_recv()
        fresh = group_sum(got) / members[...]
        change = fresh - mean[...]
        mean[...] = fresh
        for number in range(len(peers)):
            back(number).start()
        table[group_rows(me_d), :] = fresh
        res_sum[pl.ds(16 + step, 1), :] = (RHO * RHO) * jnp.sum(change * change, axis=0, keepdims=True)

        lax.fori_loop(area_count // 2, area_count, interior, 0)

        for number in range(len(peers)):
            back(number, here=True).wait_recv()
        pieces = split3(table[...])
        z_slot = mm(place[...], pieces[0]) + mm(place[...], pieces[1]) + mm(place[...], pieces[2])
        gap = (blk[...] - z_slot) * live[...]
        fresh_duals = duals[...] + gap
        duals[...] = fresh_duals
        rhs_b[...] = base_b[...] + RHO * (live[...] * (z_slot - fresh_duals))
        res_sum[pl.ds(step, 1), :] = jnp.sum(gap * gap, axis=0, keepdims=True)
        for number in range(len(peers)):
            outgoing(number, got, got_sem).wait_send()
            back(number).wait_send()
        return carry

    lax.fori_loop(0, ITERS, iterate, 0)

    def near_copy(number, here=False):
        device, _, mine, theirs = peers[number]
        at = theirs if here else mine
        return pltpu.make_async_remote_copy(
            src_ref=res_sum, dst_ref=res_near.at[at],
            send_sem=send_sem.at[number], recv_sem=near_sem.at[at], device_id=device, device_id_type=MESH,
        )

    def far_copy(number, here=False):
        device, _, mine, theirs = peers[number]
        at = (theirs if here else mine) - n_dev
        return pltpu.make_async_remote_copy(
            src_ref=res_sum, dst_ref=res_far.at[at],
            send_sem=send_sem.at[number], recv_sem=far_sem.at[at], device_id=device, device_id_type=MESH,
        )

    nears = range(n_dev - 1)
    fars = range(n_dev - 1, len(peers))
    for number in nears:
        near_copy(number).start()
    res_near[pl.ds(me_d, 1)] = res_sum[...][None]
    lane_from = lax.broadcasted_iota(jnp.int32, (BLK, BLK), 0)
    lane_to = lax.broadcasted_iota(jnp.int32, (BLK, BLK), 1)
    wanted = lax.rem(lane_to, ROWS_SLOT) * scenarios + lane_to // ROWS_SLOT
    lanes_hot = jnp.where(lane_from == wanted, 1.0, 0.0).astype(BF16)
    pieces = split3(duals[...])
    duals_ref[...] = mm(pieces[0], lanes_hot) + mm(pieces[1], lanes_hot) + mm(pieces[2], lanes_hot)
    for number in nears:
        near_copy(number, here=True).wait_recv()
        near_copy(number).wait_send()
    total = res_near[0]
    for index in range(1, n_dev):
        total = total + res_near[index]
    res_sum[...] = total
    for number in fars:
        far_copy(number).start()
    res_far[pl.ds(me_r, 1)] = total[None]
    for number in fars:
        far_copy(number, here=True).wait_recv()
        far_copy(number).wait_send()
    total = res_far[0]
    for index in range(1, n_region):
        total = total + res_far[index]
    sums = jnp.sum(total, axis=1, keepdims=True) / float(area_count * n_dev * n_region * BLK)
    lane = lax.broadcasted_iota(jnp.int32, (16, BLK), 1)
    res_ref[...] = jnp.where(lane == 0, sums[:16], sums[16:])


def on_device(loads, factor, pivots, lower, upper, incidence, counts):
    area_count, scenarios, order = loads.shape
    slots = incidence.shape[1]
    items = area_count * slots
    n_dev = lax.axis_size("dev")
    n_region = lax.axis_size("region")
    groups = n_dev + n_region
    peers = groups - 2
    table_rows = groups * BUS_DEV
    places = ROWS_SLOT * items
    rows = area_count * scenarios
    live_slot = jnp.arange(slots)[None, :] < counts[:, None]
    owner = incidence // BUS_DEV
    near = owner // n_dev == lax.axis_index("region")
    group = jnp.where(near, owner % n_dev, n_dev + owner // n_dev)
    at = jnp.where(live_slot, group * BUS_DEV + incidence % BUS_DEV, -1).astype(jnp.int32)

    vmem = pl.BlockSpec(memory_space=pltpu.VMEM)
    square = pltpu.VMEM((items, BLK), F32)
    bus = pltpu.VMEM((BUS_DEV, BLK), F32)
    listed = pltpu.VMEM((table_rows, BLK), F32)
    dma = pltpu.SemaphoreType.DMA
    dispatch, duals, res = pl.pallas_call(
        functools.partial(kernel, n_region, n_dev, area_count, scenarios, order, slots),
        out_shape=(
            jax.ShapeDtypeStruct(loads.shape, F32),
            jax.ShapeDtypeStruct((items, BLK), F32),
            jax.ShapeDtypeStruct((16, BLK), F32),
        ),
        in_specs=[vmem, pl.BlockSpec(memory_space=pl.ANY)] + [vmem] * 5,
        out_specs=(vmem, vmem, vmem),
        scratch_shapes=[
            pltpu.VMEM((area_count, order, order), BF16),
            pltpu.VMEM((order, places), BF16),
            pltpu.VMEM((rows, order), F32),
            pltpu.VMEM((rows, order), BF16),
            pltpu.VMEM((rows, order), F32),
            pltpu.VMEM((table_rows, items), BF16),
            pltpu.VMEM((items, table_rows), BF16),
            square, square, square, square, square, square, square, square, square,
            listed, listed, listed, bus, listed, bus,
            pltpu.VMEM((32, BLK), F32),
            pltpu.VMEM((n_dev, 32, BLK), F32),
            pltpu.VMEM((n_region, 32, BLK), F32),
            dma((area_count,)), dma((peers,)), dma((peers,)), dma((groups,)), dma((groups,)), dma((groups,)),
            dma((n_dev,)), dma((n_region,)),
        ],
        compiler_params=pltpu.CompilerParams(
            collective_id=0, has_side_effects=True, vmem_limit_bytes=48 * 1024 * 1024
        ),
        name="admm",
    )(loads, factor, pivots, lower, upper, at.reshape(1, items), at.reshape(items, 1))
    return dispatch, duals.reshape(area_count, slots, BLK), res[:ITERS, :2]


def solution(mesh):
    placed = (
        P(("region", "dev"), None, None),
        P(("region", "dev"), None, None),
        P(("region", "dev"), None),
        P(("region", "dev"), None),
        P(("region", "dev"), None),
        P(("region", "dev"), None),
        P(("region", "dev")),
    )
    return jax.shard_map(
        on_device,
        mesh=mesh,
        in_specs=placed,
        out_specs=(P(("region", "dev"), None, None), P(("region", "dev"), None, None), P()),
        check_vma=False,
    )
```

time: 1660 us -> 150 us (0.09); the launches traced: 1640 us -> 150 us
  blocking collectives: 536 us -> 0 us
  matrix products: 467 us -> 0 us
  starting transfers between devices: 223 us -> 0 us
  waiting for transfers between devices: 185 us -> 0 us
  Pallas kernels: 0 us -> 142 us
  other arithmetic: 130 us -> 0.76 us
  local copies, waits for them, and re-layouts: 89.1 us -> 5.9 us
    psum x14 -> x0, blocking collectives: 536 us -> none  [iterate(): partial_value = lax.psum(partial_value, ('region', 'dev'))]
    dot_general x294 -> x0, matrix products: 467 us -> none  [the longest x112 202 us: apply_inverse(): jnp.einsum('ask,aik->asi', rounded[:, :, :finish], factor[:, index_row *...]
    all_to_all x58 -> x0, starting transfers between devices: 223 us -> none  [the longest x14 70.7 us: iterate(): lax.all_to_all(z_list[far_start:], 'region', split_axis=0, concat_axis=0,...]
    all_to_all x58 -> x0, waiting for transfers between devices: 185 us -> none  [the longest x14 74.5 us: iterate(): lax.all_to_all(z_list[far_start:], 'region', split_axis=0, concat_axis=0,...]
    pallas_call x0 -> x1, Pallas kernels: none -> 142 us  [on_device(): pl.pallas_call(functools.partial(kernel, n_region, n_dev, area_count, sce...]
    another operation x43 -> x0, other arithmetic: 39.2 us -> none
    convert_element_type x42 -> x0, other arithmetic: 37.9 us -> none  [the longest x14 26.3 us: apply_inverse(): rounded = right_side.astype(jnp.bfloat16)]
    sub x16 -> x0, other arithmetic: 35.5 us -> none  [the longest x14 35.5 us: iterate(): offset = offset + dispatch - clipped_new]
  transfers between devices with their start and end apart: 58 -> 0, of which waited for: 44 -> 0; matrix products, arithmetic and copies ran while one was open for 14% -> 0% of each run, Pallas kernels for 0% -> 0%
where the time goes in v1:
time: 150 us
  Pallas kernels  142 us (95%)
  local copies, waits for them, and re-layouts  5.9 us (4%)
    pallas_call x1, Pallas kernels, on_device(): pl.pallas_call(functools.partial(kernel, n_region, n_dev, area_count, sce...  142 us
    unnamed x11, local copies, waits for them, and re-layouts  5.74 us

profile of v1, /device:TPU:0, one launch (start us, length us, event | category | flops | bytes accessed | tf_op | source)
XLA Modules:
  0.0 149.7 jit_solution(11134646886411638223)
XLA Ops:
  0.6 0.8 fusion.3
  1.4 0.1 reshape.16.row_ref
  1.5 0.1 reshape.19.col_ref
  1.6 0.0 copy-start
  1.6 1.2 copy-done
  2.8 0.0 copy-start.1
  2.8 0.8 copy-done.1
  3.6 0.0 copy-start.2
  3.6 0.8 copy-done.2
  4.3 0.0 copy-start.3
  4.3 0.8 copy-done.3
  5.1 142.4 %admm.1 = (f32[8,32,1024]{2,1,0:T(8,128)S(1)}, f32[128,128]{1,0:T(8,128)S(1)}, f32[16,128]{1,0:T(8,128)S(1)}) custom-call(f32[8,32,1024]{2,1,0:T(8,128)S(1)} %copy-done, bf16[8,1024,1024]{2,1,0:T(8,128)(2,1)} %factor_ref.1, f32[8,1024]{1,0:T(8,128)S(1)} %copy-done.1, f32[8,1024]{1,0:T(8,128)S(1)} %copy-done.2, f32[8,1024]{1,0:T(8,128)S(1)} %copy-done.3, ...), custom_call_target="tpu_custom_call" | custom-call | tf_op jit(solution)/shard_map/admm/pallas_call | solution.py:330
  147.5 0.6 copy.11
  148.1 1.0 copy.14
  149.1 0.6 copy.15
Async XLA Ops:
  1.6 1.2 copy-start
  2.8 0.8 copy-start.1
  3.6 0.8 copy-start.2
  4.3 0.8 copy-start.3

commit v2 on v1

--- a/solution.py
+++ b/solution.py
@@ -35,11 +35,11 @@
 
 def kernel(
     n_region, n_dev, area_count, scenarios, order, slots,
-    loads_ref, factor_ref, pivots_ref, lower_ref, upper_ref, row_ref, col_ref,
+    loads_hbm, factor_ref, pivots_hbm, lower_hbm, upper_hbm, row_ref, col_ref,
     dispatch_ref, duals_ref, res_ref,
-    fac, wide, known, scaled, offset, pick, place, live, rhs_b, base_b, off_b, loads_b, low_b, up_b, blk, duals,
+    loads_ref, pivots_ref, lower_ref, upper_ref, fac, wide, known, scaled, offset, pick, place, live, rhs_b, base_b, off_b, loads_b, low_b, up_b, blk, duals,
     part, got, table, mean, counts_got, members, res_sum, res_near, res_far,
-    fac_sem, send_sem, back_send, got_sem, table_sem, counts_sem, near_sem, far_sem,
+    in_sem, fac_sem, send_sem, back_send, got_sem, table_sem, counts_sem, near_sem, far_sem,
 ):
     me_r = lax.axis_index("region")
     me_d = lax.axis_index("dev")
@@ -50,12 +50,20 @@
     groups = n_dev + n_region
     near = [lax.rem(me_d + step, n_dev) for step in range(1, n_dev)]
     far = [lax.rem(me_r + step, n_region) for step in range(1, n_region)]
-    peers = [((me_r, d), d, me_d, d) for d in near]
-    peers += [((r, me_d), n_dev + r, n_dev + me_r, n_dev + r) for r in far]
+    peers = [((r, me_d), n_dev + r, n_dev + me_r, n_dev + r) for r in far]
+    peers += [((me_r, d), d, me_d, d) for d in near]
 
     def factor_copy(area):
         return pltpu.make_async_copy(factor_ref.at[area], fac.at[area], fac_sem.at[area])
 
+    inputs = [
+        pltpu.make_async_copy(held, here, in_sem.at[number])
+        for number, (held, here) in enumerate(
+            ((loads_hbm, loads_ref), (pivots_hbm, pivots_ref), (lower_hbm, lower_ref), (upper_hbm, upper_ref))
+        )
+    ]
+    for copy in inputs:
+        copy.start()
     for area in range(area_count):
         factor_copy(area).start()
 
@@ -128,6 +136,8 @@
         parts = [mm(piece, order_hot) for piece in split3(x)]
         return stack_rows(parts[0] + parts[1] + parts[2]).T
 
+    for copy in inputs:
+        copy.wait()
     loads_b[...] = to_blocks(jnp.concatenate([loads_ref[a, :, :BLK] for a in range(area_count)], axis=1))
     for bound, kept in ((lower_ref, low_b), (upper_ref, up_b)):
         line = jnp.concatenate([bound[a : a + 1, :BLK] for a in range(area_count)], axis=1)
@@ -137,13 +147,14 @@
     tiles = order // TILE
 
     def forward_known(area, pieces):
+        at = slice(area * scenarios, (area + 1) * scenarios)
         for c in range(tiles):
             here = jnp.concatenate(pieces[: c + 1], axis=1) if c else pieces[0]
-            known[pl.ds(area * scenarios, scenarios), c * TILE : (c + 1) * TILE] = mm(
+            known[at, c * TILE : (c + 1) * TILE] = mm(
                 here, fac[area, c * TILE : (c + 1) * TILE, : (c + 1) * TILE], NT
             )
 
-    def first(area, carry):
+    def first(area):
         factor_copy(area).wait()
         pieces = []
         for c in range(tiles):
@@ -152,9 +163,9 @@
                 value = jnp.where(column < edge, 0.0, value)
             pieces.append(value.astype(BF16))
         forward_known(area, pieces)
-        return carry
-
-    lax.fori_loop(0, area_count, first, 0)
+
+    for area in range(area_count):
+        first(area)
 
     def gather_wide(chunk, carry):
         at = pl.ds(pl.multiple_of(chunk * TILE, TILE), TILE)
@@ -178,23 +189,29 @@
     own_area = lax.broadcasted_iota(jnp.int32, (scenarios, places), 1)
     own_area = lax.rem(own_area // slots, area_count)
 
-    def interior(area, carry):
-        at = pl.ds(pl.multiple_of(area * scenarios, scenarios), scenarios)
+    def dispatch_of(area):
+        at = slice(area * scenarios, (area + 1) * scenarios)
         pieces = []
         for c in range(tiles):
             cols = slice(c * TILE, (c + 1) * TILE)
             found = mm(scaled[at, c * TILE :], fac[area, c * TILE :, cols])
             dispatch_ref[area, :, cols] = found
             moved = found + offset[at, cols]
-            boxed = jnp.clip(moved, lower_ref[pl.ds(area, 1), cols], upper_ref[pl.ds(area, 1), cols])
+            boxed = jnp.clip(moved, lower_ref[area : area + 1, cols], upper_ref[area : area + 1, cols])
             rest = moved - boxed
             offset[at, cols] = rest
             value = loads_ref[area, :, cols] + SIGMA * (boxed - rest)
             if c == 0:
                 value = jnp.where(column < edge, 0.0, value)
             pieces.append(value.astype(BF16))
-        forward_known(area, pieces)
-        return carry
+        return pieces
+
+    def interior(begin, finish):
+        waiting = dispatch_of(begin)
+        for area in range(begin, finish):
+            after = dispatch_of(area + 1) if area + 1 < finish else None
+            forward_known(area, waiting)
+            waiting = after
 
     def iterate(step, carry):
         turned = rhs_b[...].T
@@ -227,7 +244,7 @@
         off_b[...] = rest
         base_b[...] = loads_b[...] + SIGMA * (boxed - rest)
 
-        lax.fori_loop(0, area_count // 2, interior, 0)
+        interior(0, area_count // 2)
 
         for number in range(len(peers)):
             incoming(number, got, got_sem).wait_recv()
@@ -239,7 +256,7 @@
         table[group_rows(me_d), :] = fresh
         res_sum[pl.ds(16 + step, 1), :] = (RHO * RHO) * jnp.sum(change * change, axis=0, keepdims=True)
 
-        lax.fori_loop(area_count // 2, area_count, interior, 0)
+        interior(area_count // 2, area_count)
 
         for number in range(len(peers)):
             back(number, here=True).wait_recv()
@@ -273,8 +290,8 @@
             send_sem=send_sem.at[number], recv_sem=far_sem.at[at], device_id=device, device_id_type=MESH,
         )
 
-    nears = range(n_dev - 1)
-    fars = range(n_dev - 1, len(peers))
+    fars = range(n_region - 1)
+    nears = range(n_region - 1, len(peers))
     for number in nears:
         near_copy(number).start()
     res_near[pl.ds(me_d, 1)] = res_sum[...][None]
@@ -334,9 +351,13 @@
             jax.ShapeDtypeStruct((items, BLK), F32),
             jax.ShapeDtypeStruct((16, BLK), F32),
         ),
-        in_specs=[vmem, pl.BlockSpec(memory_space=pl.ANY)] + [vmem] * 5,
+        in_specs=[pl.BlockSpec(memory_space=pl.ANY)] * 5 + [vmem] * 2,
         out_specs=(vmem, vmem, vmem),
         scratch_shapes=[
+            pltpu.VMEM(loads.shape, F32),
+            pltpu.VMEM(pivots.shape, F32),
+            pltpu.VMEM(lower.shape, F32),
+            pltpu.VMEM(upper.shape, F32),
             pltpu.VMEM((area_count, order, order), BF16),
             pltpu.VMEM((order, places), BF16),
             pltpu.VMEM((rows, order), F32),
@@ -349,11 +370,11 @@
             pltpu.VMEM((32, BLK), F32),
             pltpu.VMEM((n_dev, 32, BLK), F32),
             pltpu.VMEM((n_region, 32, BLK), F32),
-            dma((area_count,)), dma((peers,)), dma((peers,)), dma((groups,)), dma((groups,)), dma((groups,)),
+            dma((4,)), dma((area_count,)), dma((peers,)), dma((peers,)), dma((groups,)), dma((groups,)), dma((groups,)),
             dma((n_dev,)), dma((n_region,)),
         ],
         compiler_params=pltpu.CompilerParams(
-            collective_id=0, has_side_effects=True, vmem_limit_bytes=48 * 1024 * 1024
+            collective_id=0, has_side_effects=True, vmem_limit_bytes=60 * 1024 * 1024
         ),
         name="admm",
     )(loads, factor, pivots, lower, upper, at.reshape(1, items), at.reshape(items, 1))

time: 150 us -> 156 us (1.040)
  Pallas kernels: 142 us -> 148 us
    pallas_call x1, Pallas kernels: 142 us -> 148 us  [on_device(): pl.pallas_call(functools.partial(kernel, n_region, n_dev, area_count, sce...]
    unnamed x11 -> x3, local copies, waits for them, and re-layouts: 5.74 us -> 5.11 us
where the time goes in v2:
time: 156 us
  Pallas kernels  148 us (95%)
  local copies, waits for them, and re-layouts  6.42 us (4%)
    pallas_call x1, Pallas kernels, on_device(): pl.pallas_call(functools.partial(kernel, n_region, n_dev, area_count, sce...  148 us
    unnamed x3, local copies, waits for them, and re-layouts  5.11 us

profile of v2, /device:TPU:0, one launch (start us, length us, event | category | flops | bytes accessed | tf_op | source)
XLA Modules:
  0.0 155.8 jit_solution(6392136447519088858)
XLA Ops:
  0.6 0.8 fusion.3
  1.4 0.6 reshape.16.row_ref
  2.0 0.7 reshape.19.col_ref
  2.7 148.0 %admm.1 = (f32[8,32,1024]{2,1,0:T(8,128)}, f32[128,128]{1,0:T(8,128)}, f32[16,128]{1,0:T(8,128)}) custom-call(f32[8,32,1024]{2,1,0:T(8,128)} %loads_hbm.1, bf16[8,1024,1024]{2,1,0:T(8,128)(2,1)} %factor_ref.1, f32[8,1024]{1,0:T(8,128)} %pivots_hbm.1, f32[8,1024]{1,0:T(8,128)} %lower_hbm.1, f32[8,1024]{1,0:T(8,128)} %upper_hbm.1, s32[1,128]{1,0:T(1,128)} %reshape.16.row_ref, ...), custom_call_target="tpu_custom_call" | custom-call | tf_op jit(solution)/shard_map/admm/pallas_call | solution.py:347
  150.7 1.3 copy.11
  152.0 2.3 %copy.14 = f32[8,32,1024]{2,1,0:T(8,128)} copy(f32[8,32,1024]{2,1,0:T(8,128)} %get-tuple-element.15) | data formatting | bytes 2097152
  154.4 1.5 copy.15
